TPU v7x, 32 devices: a whole 2x2x4 slice. The times are simulated.
32 devices in a mesh: lat: 4 (over y, core), lon: 8 (over z, x).
Axes of the slice: x: 2, y: 2, z: 4, core: 2. Of those that a mesh axis runs over, the one named last changes fastest.
Arguments:
- state: float32 [4, 80, 32, 1024], P(None, None, 'lat', 'lon'), may hold values from -4 to 4
- mixing: float32 [32, 1024], P('lat', 'lon'), may hold values from 0.2 to 5
- insolation: float32 [32, 1024], P('lat', 'lon'), may hold values from 0 to 1
- filter_rows: int32 [32], replicated, may hold values 0 or 1
- block_map: int32 [32, 1024], P('lat', 'lon'), may hold values from 0 to 32767, as said below
Outputs:
- state_out: float32 [4, 80, 32, 1024], P(None, None, 'lat', 'lon')
- block_heating: float32 [32, 80, 1024], P(('lat', 'lon'))
Inputs may be any that keep to these rules, and one draw needn't show every extreme that they name: `block_map`: blocks are numbered like the devices of the lat+lon axes. The 1024 columns of every device's tile give exactly 32 columns to each block, and each block's 1024 slots are each named by exactly one column.
All inputs are finite; a program needn't handle non-finite values.
Results may differ from a plain program's by a relative error of at most 0.0001.
Values sent between devices are 32-bit elements; how exact they have to be, the bound alone decides.
A program may use at most 64 MiB of HBM per device.

v0:
```python
import functools
import math

import jax
import jax.numpy as jnp
import numpy as np
from jax import lax
from jax.experimental import pallas as pl
from jax.experimental.pallas import tpu as pltpu
from jax.sharding import PartitionSpec as P

STEPS = 2
KEEP = 64
ADVECT = 0.1
DIFFUSE = 0.1
ROTATE = 0.2
RADIATE = 0.5
FLOOR = 0.25
MESH = pl.DeviceIdType.MESH
F32 = jnp.float32
BF16 = jnp.bfloat16


def filter_tables(fields, tile, n_lon, rank):
    total = tile * n_lon
    ids, waves = np.arange(tile), np.arange(KEEP)
    phase = 2 * np.pi * np.outer(ids, waves) / total
    basis = np.concatenate([np.cos(phase), np.sin(phase[:, 1:])], axis=1)
    basis = basis * np.sqrt(2 / total)
    basis[:, 0] /= np.sqrt(2)
    left = np.linalg.svd(basis, full_matrices=False)[0][:, :rank]
    between = np.zeros((n_lon, rank, n_lon, rank))
    for apart in range(-n_lon + 1, n_lon):
        gap = apart * tile + ids[:, None] - ids[None, :]
        kernel = np.ones(gap.shape) / total
        for wave in range(1, KEEP):
            kernel += (2 / total) * np.cos(2 * np.pi * ((wave * gap) % total) / total)
        block = left.T @ kernel @ left
        for source in range(n_lon):
            if 0 <= source + apart < n_lon:
                between[source, :, source + apart, :] = block.T
    lanes = fields * rank
    analysis = np.zeros((fields, tile, lanes))
    synthesis = np.zeros((lanes, fields, tile))
    for f in range(fields):
        analysis[f, :, f * rank : (f + 1) * rank] = left
        synthesis[f * rank : (f + 1) * rank, f, :] = left.T
    return (
        analysis.reshape(fields * tile, lanes).astype(np.float32),
        between.reshape(n_lon * rank, n_lon * rank).astype(np.float32),
        synthesis.reshape(lanes, fields * tile).astype(np.float32),
    )


def dot(a, b):
    return jnp.dot(a, b, precision=lax.Precision.HIGHEST, preferred_element_type=F32)


def dot_nt(a, b):
    return lax.dot_general(a, b, (((1,), (1,)), ((), ())), preferred_element_type=F32)


def split3(x):
    high = x.astype(BF16)
    rest = x - high.astype(F32)
    middle = rest.astype(BF16)
    low = (rest - middle.astype(F32)).astype(BF16)
    return high, middle, low


def kernel(
    n_lat,
    n_lon,
    state,
    mixing,
    sun,
    wanted_rows,
    block_map,
    analysis,
    between,
    synthesis,
    geometry,
    out,
    block_out,
    stepped,
    current,
    ratios,
    inverses,
    heat,
    lat_send,
    lat_recv,
    lon_send,
    lon_recv,
    z_send,
    z_recv,
    y_send,
    y_recv,
    slot_send,
    slot_recv,
    to_sorted,
    to_slots,
    heat_split,
    heat_send,
    heat_recv,
    halo_ssem,
    halo_rsem,
    z_ssem,
    z_rsem,
    y_ssem,
    y_rsem,
    slot_ssem,
    slot_rsem,
    heat_ssem,
    heat_rsem,
):
    fields, levels, rows, tile = state.shape
    n = n_lat * n_lon
    columns = rows * tile
    per_peer = columns // n
    rank = tile // fields
    share = levels // n_lon
    group = tile // fields
    groups = lon_send.shape[2]
    lat = lax.axis_index("lat")
    lon = lax.axis_index("lon")
    me = lat * n_lon + lon
    east = lax.rem(lon + 1, n_lon)
    west = lax.rem(lon + n_lon - 1, n_lon)

    barrier = pltpu.get_barrier_semaphore()

    @pl.loop(1, n)
    def _(d):
        peer = lax.rem(me + d, n)
        pl.semaphore_signal(
            barrier, inc=1, device_id=(peer // n_lon, lax.rem(peer, n_lon)), device_id_type=MESH
        )

    lane = lax.broadcasted_iota(jnp.int32, (rows, tile), 1)
    row = lax.broadcasted_iota(jnp.int32, (rows, tile), 0)
    metric = geometry[lat, 0]
    coriolis = geometry[lat, 1]
    wanted = jnp.zeros((rows, tile), jnp.int32)
    for r in range(rows):
        wanted = jnp.where(row == r, wanted_rows[lat * rows + r], wanted)
    filtered = (wanted == 1)[None]
    lon_part = lane // rank

    def halo(t, side):
        if side < 2:
            src, dst = lat_send.at[t, side], lat_recv.at[t, side]
            peer = (lat + (1 if side == 0 else -1), lon)
        else:
            src, dst = lon_send.at[t, side - 2], lon_recv.at[t, side - 2]
            peer = (lat, east if side == 2 else west)
        return pltpu.make_async_remote_copy(
            src_ref=src,
            dst_ref=dst,
            send_sem=halo_ssem.at[t, side],
            recv_sem=halo_rsem.at[t, side],
            device_id=peer,
            device_id_type=MESH,
        )

    def pack(t, src):
        for f in range(fields):
            lat_send[t, 0, f] = src[f, :, rows - 1, :]
            lat_send[t, 1, f] = src[f, :, 0, :]
        for g in range(groups):
            lon_send[t, 0, g] = jnp.zeros((rows, tile), F32)
            lon_send[t, 1, g] = jnp.zeros((rows, tile), F32)

        @pl.loop(0, levels)
        def _(l):
            g = l // group
            first = lon_send[t, 1, g]
            last = lon_send[t, 0, g]
            for f in range(fields):
                x = src[f, l]
                spot = lane == lax.rem(l, group) * fields + f
                first = jnp.where(spot, jnp.broadcast_to(x[:, :1], x.shape), first)
                last = jnp.where(spot, jnp.broadcast_to(x[:, tile - 1 :], x.shape), last)
            lon_send[t, 1, g] = first
            lon_send[t, 0, g] = last

    def start_halos(t):
        halo(t, 2).start()
        halo(t, 3).start()

        @pl.when(lat < n_lat - 1)
        def _():
            halo(t, 0).start()

        @pl.when(lat > 0)
        def _():
            halo(t, 1).start()

    def wait_halos(t):
        @pl.when(lat > 0)
        def _():
            halo(t, 0).wait_recv()

        @pl.when(lat == 0)
        def _():
            lat_recv[t, 0] = jnp.zeros(lat_recv.shape[2:], F32)

        @pl.when(lat < n_lat - 1)
        def _():
            halo(t, 1).wait_recv()

        @pl.when(lat == n_lat - 1)
        def _():
            lat_recv[t, 1] = jnp.zeros(lat_recv.shape[2:], F32)

        halo(t, 2).wait_recv()
        halo(t, 3).wait_recv()

    def wait_halo_sends(t):
        @pl.when(lat < n_lat - 1)
        def _():
            halo(t, 0).wait_send()

        @pl.when(lat > 0)
        def _():
            halo(t, 1).wait_send()

        halo(t, 2).wait_send()
        halo(t, 3).wait_send()

    def advance(t, src):
        @pl.loop(0, levels)
        def _(l):
            g = l // group
            from_west = lon_recv[t, 0, g]
            from_east = lon_recv[t, 1, g]
            u = src[0, l]
            v = src[1, l]
            zonal = u * metric
            for f in range(fields):
                x = src[f, l]
                spot = lax.rem(l, group) * fields + f
                eastern = jnp.where(
                    lane == tile - 1,
                    pltpu.roll(from_east, tile - 1 - spot, 1),
                    pltpu.roll(x, tile - 1, 1),
                )
                western = jnp.where(
                    lane == 0,
                    pltpu.roll(from_west, lax.rem(tile - spot, tile), 1),
                    pltpu.roll(x, 1, 1),
                )
                northern = jnp.where(
                    row == rows - 1, lat_recv[t, 1, f, pl.ds(l, 1), :], pltpu.roll(x, rows - 1, 0)
                )
                southern = jnp.where(row == 0, lat_recv[t, 0, f, pl.ds(l, 1), :], pltpu.roll(x, 1, 0))
                new = x - ADVECT * (zonal * (eastern - western) + v * (northern - southern))
                new = new + DIFFUSE * (eastern + western + northern + southern - 4.0 * x)
                if f == 0:
                    new = new + ROTATE * coriolis * v
                if f == 1:
                    new = new - ROTATE * coriolis * u
                stepped[f, l] = new

    def z_copy(t, d):
        owner = lax.rem(lon + d, n_lon)
        return pltpu.make_async_remote_copy(
            src_ref=z_send.at[t, d],
            dst_ref=z_recv.at[t, d],
            send_sem=z_ssem.at[t, d],
            recv_sem=z_rsem.at[t, d],
            device_id=(lat, owner),
            device_id_type=MESH,
        )

    def y_copy(t, d):
        source = lax.rem(lon + n_lon - d, n_lon)
        return pltpu.make_async_remote_copy(
            src_ref=y_send.at[t, d],
            dst_ref=y_recv.at[t, d],
            send_sem=y_ssem.at[t, d],
            recv_sem=y_rsem.at[t, d],
            device_id=(lat, source),
            device_id_type=MESH,
        )

    def analyse(t):
        @pl.loop(1, n_lon + 1)
        def _(step):
            d = lax.rem(step, n_lon)
            start = lax.rem(lon + d, n_lon) * share
            parts = [
                stepped[f, pl.ds(start, share)].reshape(share * rows, tile) for f in range(fields)
            ]
            z = dot(jnp.concatenate(parts, axis=1), analysis[...])

            @pl.when(d > 0)
            def _():
                z_send[t, d] = z.reshape(share, rows, tile)
                z_copy(t, d).start()

            @pl.when(d == 0)
            def _():
                z_recv[t, 0] = z.reshape(share, rows, tile)

    def own(t):
        @pl.loop(1, n_lon)
        def _(d):
            z_copy(t, d).wait_recv()

        count = share * rows
        wide = lax.broadcasted_iota(jnp.int32, (count, tile), 1) // rank
        halves = []
        for h in range(n_lon // fields):
            got = []
            for k in range(fields):
                d = lax.rem(lon + n_lon - (h * fields + k), n_lon)
                got.append(z_recv[t, d].reshape(count, tile))
            per_field = []
            for f in range(fields):
                total = got[0] if f == 0 else pltpu.roll(got[0], tile - rank * f, 1)
                for k in range(1, fields):
                    shift = (rank * (k - f)) % tile
                    moved = pltpu.roll(got[k], shift, 1) if shift else got[k]
                    total = jnp.where(wide == k, moved, total)
                per_field.append(total)
            halves.append(jnp.concatenate(per_field, axis=0))
        y = dot(jnp.concatenate(halves, axis=1), between[...])
        for p in range(n_lon):
            h, k = p // fields, p % fields
            total = None
            for f in range(fields):
                piece = y[f * count : (f + 1) * count, h * tile : (h + 1) * tile]
                shift = (rank * (f - k)) % tile
                piece = pltpu.roll(piece, shift, 1) if shift else piece
                total = piece if total is None else jnp.where(wide == f, piece, total)
            d = lax.rem(lon + n_lon - p, n_lon)
            total = total.reshape(share, rows, tile)

            @pl.when(d > 0)
            def _():
                y_send[t, d] = total
                y_copy(t, d).start()

            @pl.when(d == 0)
            def _():
                y_recv[t, 0] = total

    def synthesise(t):
        @pl.loop(0, n_lon)
        def _(d):
            @pl.when(d > 0)
            def _():
                y_copy(t, d).wait_recv()

            start = lax.rem(lon + d, n_lon) * share
            smooth = dot(y_recv[t, d].reshape(share * rows, tile), synthesis[...])
            for f in range(fields):
                piece = smooth[:, f * tile : (f + 1) * tile].reshape(share, rows, tile)
                here = pl.ds(start, share)
                current[f, here] = jnp.where(filtered, piece, stepped[f, here])

    def slot_copy(d):
        peer = lax.rem(me + d, n)
        return pltpu.make_async_remote_copy(
            src_ref=slot_send.at[peer],
            dst_ref=slot_recv.at[me],
            send_sem=slot_ssem.at[d],
            recv_sem=slot_rsem.at[d],
            device_id=(peer // n_lon, lax.rem(peer, n_lon)),
            device_id_type=MESH,
        )

    def heat_copy(d):
        peer = lax.rem(me + d, n)
        there = pl.ds(pl.multiple_of(peer * per_peer, per_peer), per_peer)
        here = pl.ds(pl.multiple_of(me * per_peer, per_peer), per_peer)
        return pltpu.make_async_remote_copy(
            src_ref=heat_send.at[there],
            dst_ref=heat_recv.at[here],
            send_sem=heat_ssem.at[d],
            recv_sem=heat_rsem.at[d],
            device_id=(peer // n_lon, lax.rem(peer, n_lon)),
            device_id_type=MESH,
        )

    def sort_columns():
        mapped = block_map[...].astype(F32)
        target = jnp.floor((mapped + 0.5) * (1.0 / columns))
        slot = mapped - target * columns
        slot_high = slot.astype(BF16)
        slot_low = (slot - slot_high.astype(F32)).astype(BF16)
        peers = lax.broadcasted_iota(jnp.int32, (n, tile), 0).astype(F32)
        before = lax.broadcasted_iota(jnp.int32, (tile, tile), 0)
        after = lax.broadcasted_iota(jnp.int32, (tile, tile), 1)
        earlier = (before < after).astype(F32).astype(BF16)
        positions = lax.broadcasted_iota(jnp.int32, (columns, tile), 0).astype(F32)
        places = lax.broadcasted_iota(jnp.int32, (tile, tile), 0).astype(F32)
        base = jnp.zeros((n, 1), F32)
        slots = jnp.zeros((n, tile), F32)
        for r in range(rows):
            hit = (peers == target[r : r + 1]).astype(F32)
            prefix = jnp.dot(hit.astype(BF16), earlier, preferred_element_type=F32) + base
            base = base + jnp.sum(hit, axis=1, keepdims=True)
            order = jnp.sum(hit * prefix, axis=0, keepdims=True)
            spot = target[r : r + 1] * per_peer + order
            to_sorted[:, r * tile : (r + 1) * tile] = (positions == spot).astype(F32).astype(BF16)
            named = (places == order).astype(F32)
            for part in (slot_high, slot_low):
                weighted = (named * part[r : r + 1].astype(F32)).astype(BF16)
                slots = slots + dot_nt(hit.astype(BF16), weighted)
        slot_send[...] = jnp.broadcast_to(slots[:, None, :], slot_send.shape)
        slot_recv[me] = slot_send[me]

        @pl.loop(1, n)
        def _(d):
            slot_copy(d).start()

    def place_columns():
        @pl.loop(1, n)
        def _(d):
            slot_copy(d).wait_recv()

        names = slot_recv[:, 0, :].T
        ids = lax.broadcasted_iota(jnp.int32, (per_peer, columns), 1).astype(F32)
        for source in range(n):
            column = names[:per_peer, source : source + 1]
            to_slots[source * per_peer : (source + 1) * per_peer, :] = (ids == column).astype(F32)

    def ratios_of_levels():
        mix = mixing[...]

        def body(l, upper):
            at_end = jnp.logical_or(l == 0, l == levels - 1)
            diagonal = 1.0 + jnp.where(at_end, 1.0, 2.0) * mix
            inverse = 1.0 / (diagonal + mix * upper)
            ratio = -mix * inverse
            inverses[l] = inverse
            ratios[l] = ratio
            return ratio

        lax.fori_loop(0, levels, body, jnp.zeros((rows, tile), F32))

    def mix_levels():
        mix = mixing[...]

        def forward(l, above):
            inverse = inverses[l]
            values = tuple((current[f, l] + mix * above[f]) * inverse for f in range(fields))
            for f in range(fields):
                out[f, l] = values[f]
            return values

        zeros = tuple(jnp.zeros((rows, tile), F32) for f in range(fields))
        lax.fori_loop(0, levels, forward, zeros, unroll=4)
        warming = RADIATE * sun[...]

        def backward(step, below):
            l = levels - 1 - step
            ratio = ratios[l]
            solved = tuple(out[f, l] - ratio * below[f] for f in range(fields))
            for f in range(fields):
                if f == 2:
                    warmed = solved[2] + warming * solved[3]
                    out[2, l] = warmed
                    heat[l] = warmed - current[2, l]
                else:
                    out[f, l] = solved[f]
            return solved

        lax.fori_loop(0, levels, backward, zeros, unroll=4)

    def send_heat():
        for r in range(rows):
            for k, part in enumerate(split3(heat[:, r, :])):
                heat_split[k, :levels, r * tile : (r + 1) * tile] = part
                if levels < tile:
                    heat_split[k, levels:, r * tile : (r + 1) * tile] = jnp.zeros(
                        (tile - levels, tile), BF16
                    )
        table = heat_split[...].reshape(3 * tile, columns)
        sorted3 = dot_nt(to_sorted[...], table)
        heat_send[...] = sorted3[:, :tile] + sorted3[:, tile : 2 * tile] + sorted3[:, 2 * tile :]

        @pl.loop(1, n)
        def _(d):
            heat_copy(d).start()

        mine = pl.ds(pl.multiple_of(me * per_peer, per_peer), per_peer)
        heat_recv[mine] = heat_send[mine]

    def place_heat():
        @pl.loop(1, n)
        def _(d):
            heat_copy(d).wait_recv()

        table = jnp.concatenate(split3(heat_recv[...].T), axis=0)
        placed = jnp.dot(table, to_slots[...].astype(BF16), preferred_element_type=F32)
        total = placed[:tile] + placed[tile : 2 * tile] + placed[2 * tile :]
        block_out[0] = total[:levels]

    pack(0, state)
    pl.semaphore_wait(barrier, n - 1)
    start_halos(0)
    sort_columns()
    wait_halos(0)
    advance(0, state)
    analyse(0)
    ratios_of_levels()
    own(0)
    place_columns()
    synthesise(0)
    for t in range(1, STEPS):
        pack(t, current)
        start_halos(t)
        wait_halos(t)
        advance(t, current)
        analyse(t)
        own(t)
        synthesise(t)
    mix_levels()
    send_heat()
    place_heat()

    for t in range(STEPS):
        wait_halo_sends(t)

        @pl.loop(1, n_lon)
        def _(d):
            z_copy(t, d).wait_send()
            y_copy(t, d).wait_send()

    @pl.loop(1, n)
    def _(d):
        slot_copy(d).wait_send()
        heat_copy(d).wait_send()


def per_device(n_lat, n_lon, state, mixing, insolation, filter_rows, block_map):
    fields, levels, rows, tile = state.shape
    n = n_lat * n_lon
    columns = rows * tile
    per_peer = columns // n
    rank = tile // fields
    share = levels // n_lon
    groups = -(-levels * fields // tile)
    analysis, between, synthesis = filter_tables(fields, tile, n_lon, rank)
    total_rows = rows * n_lat
    latitude = (np.arange(total_rows) + 0.5) * (math.pi / total_rows) - 0.5 * math.pi
    by_row = np.stack([1.0 / np.maximum(np.cos(latitude), FLOOR), np.sin(latitude)])
    by_row = by_row.reshape(2, n_lat, rows, 1).transpose(1, 0, 2, 3)
    geometry = np.broadcast_to(by_row, (n_lat, 2, rows, tile)).astype(np.float32)
    vmem = pl.BlockSpec(memory_space=pltpu.VMEM)
    smem = pl.BlockSpec(memory_space=pltpu.SMEM)
    block = (share, rows, tile)
    sems = pltpu.SemaphoreType.DMA
    return pl.pallas_call(
        functools.partial(kernel, n_lat, n_lon),
        out_shape=(
            jax.ShapeDtypeStruct(state.shape, F32),
            jax.ShapeDtypeStruct((1, levels, columns), F32),
        ),
        in_specs=[vmem, vmem, vmem, smem, vmem, vmem, vmem, vmem, vmem],
        out_specs=(vmem, vmem),
        scratch_shapes=[
            pltpu.VMEM(state.shape, F32),
            pltpu.VMEM(state.shape, F32),
            pltpu.VMEM((levels, rows, tile), F32),
            pltpu.VMEM((levels, rows, tile), F32),
            pltpu.VMEM((levels, rows, tile), F32),
            pltpu.VMEM((STEPS, 2, fields, levels, tile), F32),
            pltpu.VMEM((STEPS, 2, fields, levels, tile), F32),
            pltpu.VMEM((STEPS, 2, groups, rows, tile), F32),
            pltpu.VMEM((STEPS, 2, groups, rows, tile), F32),
            pltpu.VMEM((STEPS, n_lon) + block, F32),
            pltpu.VMEM((STEPS, n_lon) + block, F32),
            pltpu.VMEM((STEPS, n_lon) + block, F32),
            pltpu.VMEM((STEPS, n_lon) + block, F32),
            pltpu.VMEM((n, 8, tile), F32),
            pltpu.VMEM((n, 8, tile), F32),
            pltpu.VMEM((columns, columns), BF16),
            pltpu.VMEM((columns, columns), F32),
            pltpu.VMEM((3, tile, columns), BF16),
            pltpu.VMEM((columns, tile), F32),
            pltpu.VMEM((columns, tile), F32),
            sems((STEPS, 4)),
            sems((STEPS, 4)),
            sems((STEPS, n_lon)),
            sems((STEPS, n_lon)),
            sems((STEPS, n_lon)),
            sems((STEPS, n_lon)),
            sems((n,)),
            sems((n,)),
            sems((n,)),
            sems((n,)),
        ],
        compiler_params=pltpu.CompilerParams(
            collective_id=0, has_side_effects=True, vmem_limit_bytes=48 * 1024 * 1024
        ),
        cost_estimate=pl.CostEstimate(flops=8 * 10**9, bytes_accessed=6 * 10**6, transcendentals=0),
    )(state, mixing, insolation, filter_rows, block_map, analysis, between, synthesis, geometry)


def solution(mesh):
    n_lat, n_lon = mesh.shape["lat"], mesh.shape["lon"]
    in_specs = (P(None, None, "lat", "lon"), P("lat", "lon"), P("lat", "lon"), P(), P("lat", "lon"))
    out_specs = (P(None, None, "lat", "lon"), P(("lat", "lon"), None, None))
    return jax.shard_map(
        functools.partial(per_device, n_lat, n_lon),
        mesh=mesh,
        in_specs=in_specs,
        out_specs=out_specs,
        check_vma=False,
    )
```

profile of v0, /device:TPU:0, one launch (start us, length us, event | category | flops | bytes accessed | tf_op | source)
XLA Modules:
  0.0 106.7 jit_solution(17136880038558458440)
XLA Ops:
  0.6 0.0 copy-start
  0.6 1.3 %copy-done = f32[4,80,8,128]{3,2,1,0:T(8,128)S(1)} copy-done((f32[4,80,8,128]{3,2,1,0:T(8,128)S(1)}, f32[4,80,8,128]{3,2,1,0:T(8,128)}, u32[]{:S(2)}) %copy-start) | copy-done | bytes 1310744
  1.9 0.0 copy-start.1
  2.0 0.7 copy-done.1
  2.6 0.0 copy-start.2
  2.6 0.7 copy-done.2
  3.3 0.0 copy-start.3
  3.3 0.7 copy-done.3
  4.0 0.0 copy-start.4
  4.0 0.7 copy-done.4
  4.7 0.0 copy-start.5
  4.7 0.9 copy-done.5
  5.6 0.0 copy-start.6
  5.6 0.9 copy-done.6
  6.6 0.0 copy-start.7
  6.6 0.9 copy-done.7
  7.5 0.0 copy-start.8
  7.5 0.8 copy-done.8
  8.3 96.6 %shard_map.104 = (f32[4,80,8,128]{3,2,1,0:T(8,128)S(1)}, f32[1,80,1024]{2,1,0:T(8,128)S(1)}) custom-call(f32[4,80,8,128]{3,2,1,0:T(8,128)S(1)} %copy-done, f32[8,128]{1,0:T(8,128)S(1)} %copy-done.1, f32[8,128]{1,0:T(8,128)S(1)} %copy-done.2, s32[32]{0:T(128)S(1)} %copy-done.4, s32[8,128]{1,0:T(8,128)S(1)} %copy-done.3, f32[512,128]{1,0:T(8,128)S(1)} %copy-done.7, ...), custom_call_target="tpu_custom_call" | custom-call | flops 8000000000 | bytes 6000000 | tf_op jit(solution)/shard_map/pallas_call | solution.py:556
  104.9 1.1 copy.13
  106.0 0.7 copy.14
Async XLA Ops:
  0.6 1.3 %copy-start = (f32[4,80,8,128]{3,2,1,0:T(8,128)S(1)}, f32[4,80,8,128]{3,2,1,0:T(8,128)}, u32[]{:S(2)}) copy-start(f32[4,80,8,128]{3,2,1,0:T(8,128)} %state.1) | copy-start | bytes 3932164
  1.9 0.7 copy-start.1
  2.6 0.7 copy-start.2
  3.3 0.7 copy-start.3
  4.0 0.7 copy-start.4
  4.7 0.9 copy-start.5
  5.6 0.9 copy-start.6
  6.6 0.9 copy-start.7
  7.5 0.8 copy-start.8
where the time goes:
time: 107 us
  Pallas kernels  96.6 us (90%)
  local copies, waits for them, and re-layouts  9.41 us (9%)
    pallas_call x1, Pallas kernels, per_device(): pl.pallas_call(functools.partial(kernel, n_lat, n_lon), out_shape=(jax.Sh...  96.6 us
    unnamed x20, local copies, waits for them, and re-layouts  9.41 us

commit v1 on v0

v1 whole, which is shorter than its diff:
```python
import functools
import math

import jax
import jax.numpy as jnp
import ml_dtypes
import numpy as np
from jax import lax
from jax.experimental import pallas as pl
from jax.experimental.pallas import tpu as pltpu
from jax.sharding import PartitionSpec as P

STEPS = 2
KEEP = 64
ADVECT = 0.1
DIFFUSE = 0.1
ROTATE = 0.2
RADIATE = 0.5
FLOOR = 0.25
MESH = pl.DeviceIdType.MESH
F32 = jnp.float32
BF16 = jnp.bfloat16


def filter_tables(fields, tile, n_lon, rank):
    total = tile * n_lon
    ids, waves = np.arange(tile), np.arange(KEEP)
    phase = 2 * np.pi * np.outer(ids, waves) / total
    basis = np.concatenate([np.cos(phase), np.sin(phase[:, 1:])], axis=1)
    basis = basis * np.sqrt(2 / total)
    basis[:, 0] /= np.sqrt(2)
    left = np.linalg.svd(basis, full_matrices=False)[0][:, :rank]
    between = np.zeros((n_lon, rank, n_lon, rank))
    for apart in range(-n_lon + 1, n_lon):
        gap = apart * tile + ids[:, None] - ids[None, :]
        kernel = np.ones(gap.shape) / total
        for wave in range(1, KEEP):
            kernel += (2 / total) * np.cos(2 * np.pi * ((wave * gap) % total) / total)
        block = left.T @ kernel @ left
        for source in range(n_lon):
            if 0 <= source + apart < n_lon:
                between[source, :, source + apart, :] = block.T
    lanes = fields * rank
    analysis = np.zeros((fields, tile, lanes))
    synthesis = np.zeros((lanes, fields, tile))
    for f in range(fields):
        analysis[f, :, f * rank : (f + 1) * rank] = left
        synthesis[f * rank : (f + 1) * rank, f, :] = left.T
    analysis = parts_of(analysis.reshape(fields * tile, lanes))
    between = parts_of(between.reshape(n_lon * rank, n_lon * rank))
    high, low = parts_of(synthesis.reshape(lanes, fields * tile))
    return (
        np.concatenate(analysis, axis=1),
        np.concatenate(between, axis=1),
        np.concatenate([high, high, low], axis=0),
    )


def parts_of(table):
    high = table.astype(ml_dtypes.bfloat16)
    return high, (table - high.astype(np.float64)).astype(ml_dtypes.bfloat16)


def split2(x):
    high = x.astype(BF16)
    return high, (x - high.astype(F32)).astype(BF16)


def dot(a, b):
    return jnp.dot(a, b, preferred_element_type=F32)


def dot_parts(x, table):
    width = table.shape[1] // 2
    high, low = split2(x)
    both = dot(high, table[...])
    return both[:, :width] + both[:, width:] + dot(low, table[:, :width])


def dot_nt(a, b):
    return lax.dot_general(a, b, (((1,), (1,)), ((), ())), preferred_element_type=F32)


def split3(x):
    high = x.astype(BF16)
    rest = x - high.astype(F32)
    middle = rest.astype(BF16)
    low = (rest - middle.astype(F32)).astype(BF16)
    return high, middle, low


def kernel(
    n_lat,
    n_lon,
    batches,
    state_in,
    mixing_in,
    sun_in,
    rows_in,
    map_in,
    analysis_in,
    between_in,
    synthesis_in,
    geometry_in,
    out,
    block_out,
    state,
    mixing,
    sun,
    wanted_rows,
    block_map,
    analysis,
    between,
    synthesis,
    geometry,
    in_sem,
    stepped,
    current,
    ratios,
    inverses,
    heat,
    to_sorted,
    to_slots,
    heat_split,
    heat_send,
    heat_recv,
    slot_send,
    slot_recv,
    slot_ssem,
    slot_rsem,
    heat_ssem,
    heat_rsem,
    *batch_refs,
):
    fields, levels, rows, tile = state.shape
    n = n_lat * n_lon
    columns = rows * tile
    per_peer = columns // n
    rank = tile // fields
    group = tile // fields
    wire = heat_send.shape[0] // n
    lat = lax.axis_index("lat")
    lon = lax.axis_index("lon")
    me = lat * n_lon + lon
    east = lax.rem(lon + 1, n_lon)
    west = lax.rem(lon + n_lon - 1, n_lon)

    sources = (
        state_in,
        mixing_in,
        sun_in,
        rows_in,
        map_in,
        analysis_in,
        between_in,
        synthesis_in,
        geometry_in,
    )
    places = (state, mixing, sun, wanted_rows, block_map, analysis, between, synthesis, geometry)
    loads = [
        pltpu.make_async_copy(src, dst, in_sem.at[k])
        for k, (src, dst) in enumerate(zip(sources, places))
    ]
    for load in loads:
        load.start()

    barrier = pltpu.get_barrier_semaphore()

    @pl.loop(1, n)
    def _(d):
        peer = lax.rem(me + d, n)
        pl.semaphore_signal(
            barrier, inc=1, device_id=(peer // n_lon, lax.rem(peer, n_lon)), device_id_type=MESH
        )

    lane = lax.broadcasted_iota(jnp.int32, (rows, tile), 1)
    row = lax.broadcasted_iota(jnp.int32, (rows, tile), 0)

    class Batch:
        pass

    def make_batch(b):
        first, share = batches[b]
        count = share * n_lon
        (
            lat_send,
            lat_recv,
            lon_send,
            lon_recv,
            z_send,
            z_recv,
            y_send,
            y_recv,
            halo_ssem,
            halo_rsem,
            z_ssem,
            z_rsem,
            y_ssem,
            y_rsem,
        ) = batch_refs[b * 14 : (b + 1) * 14]
        groups = lon_send.shape[2]
        here = pl.ds(first, count)
        many = share * rows

        def halo(t, side):
            if side < 2:
                src, dst = lat_send.at[t, side], lat_recv.at[t, side]
                peer = (lat + (1 if side == 0 else -1), lon)
            else:
                src, dst = lon_send.at[t, side - 2], lon_recv.at[t, side - 2]
                peer = (lat, east if side == 2 else west)
            return pltpu.make_async_remote_copy(
                src_ref=src,
                dst_ref=dst,
                send_sem=halo_ssem.at[t, side],
                recv_sem=halo_rsem.at[t, side],
                device_id=peer,
                device_id_type=MESH,
            )

        def pack(t, src):
            for f in range(fields):
                lat_send[t, 0, f] = src[f, here, rows - 1, :]
                lat_send[t, 1, f] = src[f, here, 0, :]
            for g in range(groups):
                lon_send[t, 0, g] = jnp.zeros((rows, tile), F32)
                lon_send[t, 1, g] = jnp.zeros((rows, tile), F32)
            chunk = math.gcd(math.gcd(count, group), 8)

            @pl.loop(0, count // chunk)
            def _(c):
                g = c * chunk // group
                low = lon_send[t, 1, g]
                high = lon_send[t, 0, g]
                for k in range(chunk):
                    l = c * chunk + k
                    for f in range(fields):
                        x = src[f, first + l]
                        spot = lane == lax.rem(l, group) * fields + f
                        low = jnp.where(spot, jnp.broadcast_to(x[:, :1], x.shape), low)
                        high = jnp.where(spot, jnp.broadcast_to(x[:, tile - 1 :], x.shape), high)
                lon_send[t, 1, g] = low
                lon_send[t, 0, g] = high

        def start_halos(t):
            halo(t, 2).start()
            halo(t, 3).start()

            @pl.when(lat < n_lat - 1)
            def _():
                halo(t, 0).start()

            @pl.when(lat > 0)
            def _():
                halo(t, 1).start()

        def wait_halos(t):
            @pl.when(lat > 0)
            def _():
                halo(t, 0).wait_recv()

            @pl.when(lat == 0)
            def _():
                lat_recv[t, 0] = jnp.zeros(lat_recv.shape[2:], F32)

            @pl.when(lat < n_lat - 1)
            def _():
                halo(t, 1).wait_recv()

            @pl.when(lat == n_lat - 1)
            def _():
                lat_recv[t, 1] = jnp.zeros(lat_recv.shape[2:], F32)

            halo(t, 2).wait_recv()
            halo(t, 3).wait_recv()

        def wait_halo_sends(t):
            @pl.when(lat < n_lat - 1)
            def _():
                halo(t, 0).wait_send()

            @pl.when(lat > 0)
            def _():
                halo(t, 1).wait_send()

            halo(t, 2).wait_send()
            halo(t, 3).wait_send()

        def advance(t, src):
            metric = geometry[lat, 0]
            coriolis = geometry[lat, 1]

            def one(l):
                g = l // group
                from_west = lon_recv[t, 0, g]
                from_east = lon_recv[t, 1, g]
                u = src[0, first + l]
                v = src[1, first + l]
                zonal = u * metric
                made = []
                for f in range(fields):
                    x = src[f, first + l]
                    spot = lax.rem(l, group) * fields + f
                    eastern = jnp.where(
                        lane == tile - 1,
                        pltpu.roll(from_east, tile - 1 - spot, 1),
                        pltpu.roll(x, tile - 1, 1),
                    )
                    western = jnp.where(
                        lane == 0,
                        pltpu.roll(from_west, lax.rem(tile - spot, tile), 1),
                        pltpu.roll(x, 1, 1),
                    )
                    northern = jnp.where(
                        row == rows - 1,
                        lat_recv[t, 1, f, pl.ds(l, 1), :],
                        pltpu.roll(x, rows - 1, 0),
                    )
                    southern = jnp.where(
                        row == 0, lat_recv[t, 0, f, pl.ds(l, 1), :], pltpu.roll(x, 1, 0)
                    )
                    new = x - ADVECT * (zonal * (eastern - western) + v * (northern - southern))
                    new = new + DIFFUSE * (eastern + western + northern + southern - 4.0 * x)
                    if f == 0:
                        new = new + ROTATE * coriolis * v
                    if f == 1:
                        new = new - ROTATE * coriolis * u
                    made.append(new)
                return made

            chunk = math.gcd(count, 4)

            @pl.loop(0, count // chunk)
            def _(c):
                made = [one(c * chunk + k) for k in range(chunk)]
                for k in range(chunk):
                    for f in range(fields):
                        stepped[f, first + c * chunk + k] = made[k][f]

        def z_copy(t, d):
            owner = lax.rem(lon + d, n_lon)
            return pltpu.make_async_remote_copy(
                src_ref=z_send.at[t, owner],
                dst_ref=z_recv.at[t, lon],
                send_sem=z_ssem.at[t, d],
                recv_sem=z_rsem.at[t, d],
                device_id=(lat, owner),
                device_id_type=MESH,
            )

        def y_copy(t, d):
            source = lax.rem(lon + d, n_lon)
            return pltpu.make_async_remote_copy(
                src_ref=y_send.at[t, source],
                dst_ref=y_recv.at[t, lon],
                send_sem=y_ssem.at[t, d],
                recv_sem=y_rsem.at[t, d],
                device_id=(lat, source),
                device_id_type=MESH,
            )

        def analyse(t):
            parts = [stepped[f, here].reshape(count * rows, tile) for f in range(fields)]
            z = dot_parts(jnp.concatenate(parts, axis=1), analysis)
            z_send[t] = z.reshape(n_lon, share, rows, tile)

            @pl.loop(1, n_lon)
            def _(d):
                z_copy(t, d).start()

            z_recv[t, lon] = z_send[t, lon]

        def own(t):
            @pl.loop(1, n_lon)
            def _(d):
                z_copy(t, d).wait_recv()

            wide = lax.broadcasted_iota(jnp.int32, (many, tile), 1) // rank
            halves = []
            for h in range(n_lon // fields):
                got = [z_recv[t, h * fields + k].reshape(many, tile) for k in range(fields)]
                per_field = []
                for f in range(fields):
                    total = None
                    for k in range(fields):
                        shift = (rank * (k - f)) % tile
                        moved = pltpu.roll(got[k], shift, 1) if shift else got[k]
                        total = moved if k == 0 else jnp.where(wide == k, moved, total)
                    per_field.append(total)
                halves.append(jnp.concatenate(per_field, axis=0))
            y = dot_parts(jnp.concatenate(halves, axis=1), between)
            for p in range(n_lon):
                h, k = p // fields, p % fields
                total = None
                for f in range(fields):
                    piece = y[f * many : (f + 1) * many, h * tile : (h + 1) * tile]
                    shift = (rank * (f - k)) % tile
                    piece = pltpu.roll(piece, shift, 1) if shift else piece
                    total = piece if f == 0 else jnp.where(wide == f, piece, total)
                y_send[t, p] = total.reshape(share, rows, tile)

            @pl.loop(1, n_lon)
            def _(d):
                y_copy(t, d).start()

            y_recv[t, lon] = y_send[t, lon]

        def synthesise(t):
            wanted = jnp.zeros((rows, tile), jnp.int32)
            for r in range(rows):
                wanted = jnp.where(row == r, wanted_rows[lat * rows + r], wanted)
            filtered = (wanted == 1)[None]

            @pl.loop(1, n_lon)
            def _(d):
                y_copy(t, d).wait_recv()

            high, low = split2(y_recv[t].reshape(count * rows, tile))
            smooth = dot(jnp.concatenate([high, low, high], axis=1), synthesis[...])
            for f in range(fields):
                piece = smooth[:, f * tile : (f + 1) * tile].reshape(count, rows, tile)
                current[f, here] = jnp.where(filtered, piece, stepped[f, here])

        def wait_sends(t):
            wait_halo_sends(t)

            @pl.loop(1, n_lon)
            def _(d):
                z_copy(t, d).wait_send()
                y_copy(t, d).wait_send()

        batch = Batch()
        batch.first, batch.count = first, count
        batch.pack, batch.start_halos, batch.wait_halos = pack, start_halos, wait_halos
        batch.advance, batch.analyse, batch.own = advance, analyse, own
        batch.synthesise, batch.wait_sends = synthesise, wait_sends
        return batch

    def slot_copy(d):
        peer = lax.rem(me + d, n)
        return pltpu.make_async_remote_copy(
            src_ref=slot_send.at[peer],
            dst_ref=slot_recv.at[me],
            send_sem=slot_ssem.at[d],
            recv_sem=slot_rsem.at[d],
            device_id=(peer // n_lon, lax.rem(peer, n_lon)),
            device_id_type=MESH,
        )

    def heat_copy(d):
        peer = lax.rem(me + d, n)
        there = pl.ds(pl.multiple_of(peer * wire, wire), wire)
        here = pl.ds(pl.multiple_of(me * wire, wire), wire)
        return pltpu.make_async_remote_copy(
            src_ref=heat_send.at[there],
            dst_ref=heat_recv.at[here],
            send_sem=heat_ssem.at[d],
            recv_sem=heat_rsem.at[d],
            device_id=(peer // n_lon, lax.rem(peer, n_lon)),
            device_id_type=MESH,
        )

    def sort_columns():
        mapped = block_map[...].astype(F32)
        target = jnp.floor((mapped + 0.5) * (1.0 / columns))
        slot = mapped - target * columns
        slot_high = slot.astype(BF16)
        slot_low = (slot - slot_high.astype(F32)).astype(BF16)
        peers = lax.broadcasted_iota(jnp.int32, (n, tile), 0).astype(F32)
        before = lax.broadcasted_iota(jnp.int32, (tile, tile), 0)
        after = lax.broadcasted_iota(jnp.int32, (tile, tile), 1)
        earlier = (before < after).astype(F32).astype(BF16)
        positions = lax.broadcasted_iota(jnp.int32, (columns, tile), 0).astype(F32)
        places = lax.broadcasted_iota(jnp.int32, (tile, tile), 0).astype(F32)
        base = jnp.zeros((n, 1), F32)
        slots = jnp.zeros((n, tile), F32)
        for r in range(rows):
            hit = (peers == target[r : r + 1]).astype(F32)
            prefix = dot(hit.astype(BF16), earlier) + base
            base = base + jnp.sum(hit, axis=1, keepdims=True)
            order = jnp.sum(hit * prefix, axis=0, keepdims=True)
            spot = target[r : r + 1] * per_peer + order
            to_sorted[:, r * tile : (r + 1) * tile] = (positions == spot).astype(F32).astype(BF16)
            named = (places == order).astype(F32)
            for part in (slot_high, slot_low):
                weighted = (named * part[r : r + 1].astype(F32)).astype(BF16)
                slots = slots + dot_nt(hit.astype(BF16), weighted)
        slot_send[...] = jnp.broadcast_to(slots[:, None, :], slot_send.shape)
        slot_recv[me] = slot_send[me]

        @pl.loop(1, n)
        def _(d):
            slot_copy(d).start()

    def place_columns():
        @pl.loop(1, n)
        def _(d):
            slot_copy(d).wait_recv()

        names = slot_recv[:, 0, :].T[:per_peer]
        join = max(1, 16 // per_peer)
        size = join * per_peer
        ids = lax.broadcasted_iota(jnp.int32, (size, columns), 1).astype(F32)
        for k in range(n // join):
            picked = [names[:, s : s + 1] for s in range(k * join, (k + 1) * join)]
            column = picked[0] if join == 1 else jnp.concatenate(picked, axis=0)
            to_slots[k * size : (k + 1) * size, :] = (ids == column).astype(F32).astype(BF16)

    def ratios_of_levels():
        mix = mixing[...]

        def body(l, upper):
            at_end = jnp.logical_or(l == 0, l == levels - 1)
            diagonal = 1.0 + jnp.where(at_end, 1.0, 2.0) * mix
            inverse = 1.0 / (diagonal + mix * upper)
            ratio = -mix * inverse
            inverses[l] = inverse
            ratios[l] = ratio
            return ratio

        lax.fori_loop(0, levels, body, jnp.zeros((rows, tile), F32))

    zeros = tuple(jnp.zeros((rows, tile), F32) for f in range(fields))

    def mix_down(batch, carried):
        mix = mixing[...]

        def forward(l, above):
            inverse = inverses[l]
            values = tuple((current[f, l] + mix * above[f]) * inverse for f in range(fields))
            for f in range(fields):
                out[f, l] = values[f]
            return values

        return lax.fori_loop(batch.first, batch.first + batch.count, forward, carried, unroll=8)

    def mix_up():
        warming = RADIATE * sun[...]

        def backward(step, below):
            l = levels - 1 - step
            ratio = ratios[l]
            solved = tuple(out[f, l] - ratio * below[f] for f in range(fields))
            for f in range(fields):
                if f == 2:
                    warmed = solved[2] + warming * solved[3]
                    out[2, l] = warmed
                    heat[l] = warmed - current[2, l]
                else:
                    out[f, l] = solved[f]
            return solved

        lax.fori_loop(0, levels, backward, zeros, unroll=8)

    spill = per_peer - wire
    half = levels // 2

    def send_heat():
        for r in range(rows):
            for k, part in enumerate(split3(heat[:, r, :])):
                heat_split[k, :levels, r * tile : (r + 1) * tile] = part
                if levels < tile:
                    heat_split[k, levels:, r * tile : (r + 1) * tile] = jnp.zeros(
                        (tile - levels, tile), BF16
                    )
        table = heat_split[...].reshape(3 * tile, columns)
        sorted3 = dot_nt(to_sorted[...], table)
        sent = sorted3[:, :tile] + sorted3[:, tile : 2 * tile] + sorted3[:, 2 * tile :]
        if spill:
            spots = lax.broadcasted_iota(jnp.int32, (spill, tile), 1)
            free = spots >= levels
            pieces = []
            for p in range(n):
                base = p * per_peer
                extra = sent[base + wire : base + per_peer]
                pieces.append(
                    jnp.where(free, pltpu.roll(extra, levels, 1), sent[base : base + spill])
                )
                pieces.append(
                    jnp.where(
                        free,
                        pltpu.roll(extra, levels - half, 1),
                        sent[base + spill : base + 2 * spill],
                    )
                )
                pieces.append(sent[base + 2 * spill : base + wire])
            sent = jnp.concatenate(pieces, axis=0)
        heat_send[...] = sent

        @pl.loop(1, n)
        def _(d):
            heat_copy(d).start()

        mine = pl.ds(pl.multiple_of(me * wire, wire), wire)
        heat_recv[mine] = heat_send[mine]

    def place_heat():
        @pl.loop(1, n)
        def _(d):
            heat_copy(d).wait_recv()

        got = heat_recv[...]
        if spill:
            spots = lax.broadcasted_iota(jnp.int32, (spill, tile), 1)
            pieces = []
            for p in range(n):
                message = got[p * wire : (p + 1) * wire]
                extra = jnp.where(
                    spots < half,
                    pltpu.roll(message[:spill], tile - levels, 1),
                    pltpu.roll(message[spill : 2 * spill], tile - levels + half, 1),
                )
                pieces += [message, extra]
            got = jnp.concatenate(pieces, axis=0)
        table = jnp.concatenate(split3(got.T), axis=0)
        placed = dot(table, to_slots[...])
        total = placed[:tile] + placed[tile : 2 * tile] + placed[2 * tile :]
        block_out[0] = total[:levels]

    work = [make_batch(b) for b in range(len(batches))]
    loads[0].wait()
    for batch in work:
        batch.pack(0, state)
    pl.semaphore_wait(barrier, n - 1)
    for batch in work:
        batch.start_halos(0)
    for load in loads[1:]:
        load.wait()
    sort_columns()
    for t in range(STEPS):
        source = state if t == 0 else current
        for batch in work:
            batch.wait_halos(t)
            batch.advance(t, source)
            batch.analyse(t)
        if t == 0:
            ratios_of_levels()
        for batch in work:
            batch.own(t)
        if t == 0:
            place_columns()
        carried = zeros
        for batch in work:
            batch.synthesise(t)
            if t + 1 < STEPS:
                batch.pack(t + 1, current)
                batch.start_halos(t + 1)
            else:
                carried = mix_down(batch, carried)
    mix_up()
    send_heat()
    for batch in work:
        for t in range(STEPS):
            batch.wait_sends(t)
    place_heat()

    @pl.loop(1, n)
    def _(d):
        slot_copy(d).wait_send()
        heat_copy(d).wait_send()


def per_device(n_lat, n_lon, state, mixing, insolation, filter_rows, block_map):
    fields, levels, rows, tile = state.shape
    n = n_lat * n_lon
    columns = rows * tile
    per_peer = columns // n
    rank = tile // fields
    share = levels // n_lon
    large = share - share // 2
    batches = ((0, large), (large * n_lon, share - large))
    analysis, between, synthesis = filter_tables(fields, tile, n_lon, rank)
    total_rows = rows * n_lat
    latitude = (np.arange(total_rows) + 0.5) * (math.pi / total_rows) - 0.5 * math.pi
    by_row = np.stack([1.0 / np.maximum(np.cos(latitude), FLOOR), np.sin(latitude)])
    by_row = by_row.reshape(2, n_lat, rows, 1).transpose(1, 0, 2, 3)
    geometry = np.broadcast_to(by_row, (n_lat, 2, rows, tile)).astype(np.float32)
    spare = per_peer % 32 == 0 and levels % 2 == 0 and levels + levels // 2 <= tile
    wire = per_peer * 3 // 4 if spare else per_peer
    vmem = pl.BlockSpec(memory_space=pltpu.VMEM)
    anywhere = pl.BlockSpec(memory_space=pl.ANY)
    sems = pltpu.SemaphoreType.DMA
    operands = (
        state,
        mixing,
        insolation,
        filter_rows,
        block_map,
        analysis,
        between,
        synthesis,
        geometry,
    )
    places = [
        pltpu.SMEM(a.shape, a.dtype) if a is filter_rows else pltpu.VMEM(a.shape, a.dtype)
        for a in operands
    ]
    per_batch = []
    for _, part in batches:
        count = part * n_lon
        edge = (STEPS, 2, fields, count, tile)
        side = (STEPS, 2, -(-count * fields // tile), rows, tile)
        block = (STEPS, n_lon, part, rows, tile)
        for shape in (edge, edge, side, side, block, block, block, block):
            per_batch.append(pltpu.VMEM(shape, F32))
        per_batch += [sems((STEPS, 4))] * 2 + [sems((STEPS, n_lon))] * 4
    return pl.pallas_call(
        functools.partial(kernel, n_lat, n_lon, batches),
        out_shape=(
            jax.ShapeDtypeStruct(state.shape, F32),
            jax.ShapeDtypeStruct((1, levels, columns), F32),
        ),
        in_specs=[anywhere] * len(operands),
        out_specs=(vmem, vmem),
        scratch_shapes=places
        + [
            sems((len(operands),)),
            pltpu.VMEM(state.shape, F32),
            pltpu.VMEM(state.shape, F32),
            pltpu.VMEM((levels, rows, tile), F32),
            pltpu.VMEM((levels, rows, tile), F32),
            pltpu.VMEM((levels, rows, tile), F32),
            pltpu.VMEM((columns, columns), BF16),
            pltpu.VMEM((columns, columns), BF16),
            pltpu.VMEM((3, tile, columns), BF16),
            pltpu.VMEM((n * wire, tile), F32),
            pltpu.VMEM((n * wire, tile), F32),
            pltpu.VMEM((n, 8, tile), F32),
            pltpu.VMEM((n, 8, tile), F32),
            sems((n,)),
            sems((n,)),
            sems((n,)),
            sems((n,)),
        ]
        + per_batch,
        compiler_params=pltpu.CompilerParams(
            collective_id=0, has_side_effects=True, vmem_limit_bytes=56 * 1024 * 1024
        ),
        cost_estimate=pl.CostEstimate(flops=8 * 10**9, bytes_accessed=6 * 10**6, transcendentals=0),
    )(*operands)


def solution(mesh):
    n_lat, n_lon = mesh.shape["lat"], mesh.shape["lon"]
    in_specs = (P(None, None, "lat", "lon"), P("lat", "lon"), P("lat", "lon"), P(), P("lat", "lon"))
    out_specs = (P(None, None, "lat", "lon"), P(("lat", "lon"), None, None))
    return jax.shard_map(
        functools.partial(per_device, n_lat, n_lon),
        mesh=mesh,
        in_specs=in_specs,
        out_specs=out_specs,
        check_vma=False,
    )
```

time: 107 us -> 70.8 us (0.66)
  Pallas kernels: 96.6 us -> 66.8 us
  local copies, waits for them, and re-layouts: 9.41 us -> 3.23 us
    pallas_call x1, Pallas kernels: 96.6 us -> 66.8 us  [per_device(): pl.pallas_call(functools.partial(kernel, n_lat, n_lon, batches), out_shap...]
    unnamed x20 -> x4, local copies, waits for them, and re-layouts: 9.41 us -> 3.23 us
where the time goes in v1:
time: 70.8 us; the launch traced here: 70.6 us
  Pallas kernels  66.8 us (94%)
  local copies, waits for them, and re-layouts  3.23 us (5%)
    pallas_call x1, Pallas kernels, per_device(): pl.pallas_call(functools.partial(kernel, n_lat, n_lon, batches), out_shap...  66.8 us
    unnamed x4, local copies, waits for them, and re-layouts  3.23 us

profile of v1, /device:TPU:0, one launch (start us, length us, event | category | flops | bytes accessed | tf_op | source)
XLA Modules:
  0.0 70.6 jit_solution(2077872943356620023)
XLA Ops:
  0.6 66.8 %shard_map.104 = (f32[4,80,8,128]{3,2,1,0:T(8,128)}, f32[1,80,1024]{2,1,0:T(8,128)}) custom-call(f32[4,80,8,128]{3,2,1,0:T(8,128)} %state_in.1, f32[8,128]{1,0:T(8,128)} %mixing_in.1, f32[8,128]{1,0:T(8,128)} %sun_in.1, s32[32]{0:T(128)} %rows_in.1, s32[8,128]{1,0:T(8,128)} %map_in.1, bf16[512,256]{1,0:T(8,128)(2,1)} %constant.8.clone.analysis_in, ...), custom_call_target="tpu_custom_call" | custom-call | flops 8000000000 | bytes 6000000 | tf_op jit(solution)/shard_map/pallas_call | solution.py:707
  67.4 0.0 copy-start
  67.4 2.5 %copy.13 = f32[4,80,8,128]{3,2,1,0:T(8,128)} copy(f32[4,80,8,128]{3,2,1,0:T(8,128)} %get-tuple-element.4) | data formatting | bytes 2621440
  69.9 0.0 copy-done
  69.9 0.7 %copy.14 = f32[1,80,1024]{2,1,0:T(8,128)} copy(f32[1,80,1024]{2,1,0:T(8,128)S(1)} %copy-done) | data formatting | bytes 655360
Async XLA Ops:
  67.4 2.5 %copy-start = (f32[1,80,1024]{2,1,0:T(8,128)S(1)}, f32[1,80,1024]{2,1,0:T(8,128)}, u32[]{:S(2)}) copy-start(f32[1,80,1024]{2,1,0:T(8,128)} %get-tuple-element.5) | copy-start | bytes 983044
